TPU v7x, 32 devices: a whole 2x2x4 slice. The times are simulated.
32 devices in a mesh: groups: 2 (over x), wide: 16 (over z, y, core).
Axes of the slice: x: 2, y: 2, z: 4, core: 2. Of those that a mesh axis runs over, the one named last changes fastest.
Arguments:
- picture_feature_maps: bfloat16 [256, 10, 10, 1536], P(('groups', 'wide')), parts along dimension 0, may hold values from -6 to 6
- partitioned_filter_tensor: bfloat16 [3, 3, 128, 1536], replicated, may hold values from -0.1875 to 0.1875
- picture_token_layer_scaling: float32 [1536], replicated, may hold values from 0.1 to 1.9
- summary_probes: bfloat16 [64, 1536], replicated, may hold values from -6 to 6
- summary_probe_layer_scaling: float32 [1536], replicated, may hold values from 0.1 to 1.9
- asking_projection_tensor: bfloat16 [1536, 1536], P('wide'), may hold values from -0.15625 to 0.15625
- lookup_projection_tensor: bfloat16 [1536, 1536], P('wide'), may hold values from -0.15625 to 0.15625
- content_projection_tensor: bfloat16 [1536, 1536], P('wide'), may hold values from -0.15625 to 0.15625
- final_projection_tensor: bfloat16 [1536, 1536], P(None, 'wide'), may hold values from -0.15625 to 0.15625
- sharpness_coefficient: float32 [16], replicated, may hold values from 0.5 to 64
Outputs:
- attended: float32 [128, 1536], P('groups'), parts along dimension 0
- new_latents: bfloat16 [128, 1536], P('groups'), parts along dimension 0
There are 2 independent parts, one for each index of `groups`. A program takes and returns all parts, laid end to end along the dimension named above; an argument that names none is the same for every part. Nothing has to cross between parts.
All inputs are finite; a program needn't handle non-finite values.
Results may differ from a plain program's by a relative error of at most 0.004.
The roundings to bfloat16 on the way count: a program that leaves them out, or rounds other values in their place, can miss the bound.
Values may be sent and summed in bfloat16 or wider, within the bound.
A program may use at most 128 MiB of HBM per device.

v0:
```python
import math
import jax
import jax.numpy as jnp
from jax import lax
from jax.sharding import PartitionSpec as P

RESIDUAL_SCALE = 0.2
EPSILON = 1e-06


def layer_norm(values, gain):
    center = values - jnp.mean(values, axis=-1, keepdims=True)
    spread = jnp.mean(center * center, axis=-1, keepdims=True)
    return center * lax.rsqrt(spread + EPSILON) * gain


def combine(left_side, right_side):
    left_max, left_sum, left_weighted = left_side
    right_max, right_sum, right_weighted = right_side
    joint_max = jnp.maximum(left_max, right_max)
    scale_left = jnp.exp(left_max - joint_max)
    scale_right = jnp.exp(right_max - joint_max)
    return (
        joint_max,
        left_sum * scale_left + right_sum * scale_right,
        left_weighted * scale_left[..., None] + right_weighted * scale_right[..., None],
    )


def merge_all(row_max, row_sum, weighted):
    joint_max = lax.pmax(row_max, "wide")
    factor = jnp.exp(row_max - joint_max)
    joint_sum, joint_weighted = lax.psum((row_sum * factor, weighted * factor[..., None]), "wide")
    return (joint_max, joint_sum, joint_weighted)


def softmax_terms(scores, carried):
    row_max = jnp.max(scores, axis=-1)
    weights = jnp.exp(scores - row_max[..., None])
    row_sum = jnp.sum(weights, axis=-1)
    weighted = jnp.einsum("hlt,thd->hld", weights, carried, precision=lax.Precision.HIGHEST)
    return (row_max, row_sum, weighted)


def per_device(
    picture_feature_maps,
    partitioned_filter_tensor,
    picture_token_layer_scaling,
    summary_probes,
    summary_probe_layer_scaling,
    asking_projection_tensor,
    lookup_projection_tensor,
    content_projection_tensor,
    final_projection_tensor,
    sharpness_coefficient,
):
    channels = picture_feature_maps.shape[3]
    subspace_number_overall = sharpness_coefficient.shape[0]
    subspace_breadth = channels // subspace_number_overall
    lat_count = summary_probes.shape[0]
    activated = jax.nn.gelu(picture_feature_maps.astype(jnp.float32)).astype(jnp.bfloat16)
    convolved = lax.conv_general_dilated(
        activated,
        partitioned_filter_tensor,
        (1, 1),
        "SAME",
        dimension_numbers=("NHWC", "HWIO", "NHWC"),
        feature_group_count=channels // partitioned_filter_tensor.shape[2],
        preferred_element_type=jnp.float32,
    )
    summed = picture_feature_maps.astype(jnp.float32) + RESIDUAL_SCALE * convolved
    tok_norm = layer_norm(summed.reshape(-1, channels), picture_token_layer_scaling).astype(
        jnp.bfloat16
    )
    lat_norm = layer_norm(summary_probes.astype(jnp.float32), summary_probe_layer_scaling).astype(
        jnp.bfloat16
    )
    tok_count = tok_norm.shape[0]
    shard_rows = asking_projection_tensor.shape[0]
    first_row = lax.axis_index("wide") * shard_rows
    lat_slice = lax.dynamic_slice_in_dim(lat_norm, first_row, shard_rows, 1)
    probe_asking_vectors = lax.psum(
        jnp.dot(lat_slice, asking_projection_tensor, preferred_element_type=jnp.float32), "wide"
    )
    rescaled_similarity_logits = (
        probe_asking_vectors.reshape(lat_count, subspace_number_overall, subspace_breadth)
        * (sharpness_coefficient / math.sqrt(subspace_breadth))[None, :, None]
    )
    key_source = jnp.concatenate([tok_norm, lat_norm], axis=0)
    zero_rows = jnp.zeros((key_source.shape[0], channels), jnp.float32)

    def add_rows(running, weight_rows):
        return running + jnp.dot(key_source, weight_rows, preferred_element_type=jnp.float32)

    def scores_of(key_part):
        return jnp.einsum(
            "lhd,thd->hlt",
            rescaled_similarity_logits,
            key_part.reshape(-1, subspace_number_overall, subspace_breadth),
            precision=lax.Precision.HIGHEST,
        )

    running = (zero_rows, zero_rows)
    weight_rows = (
        lax.all_gather(lookup_projection_tensor, "wide", axis=0, tiled=True),
        lax.all_gather(content_projection_tensor, "wide", axis=0, tiled=True),
    )
    key_proj = add_rows(running[0], weight_rows[0])
    value_proj = add_rows(running[1], weight_rows[1])
    tok_terms = softmax_terms(
        scores_of(key_proj[:tok_count]),
        value_proj[:tok_count].reshape(-1, subspace_number_overall, subspace_breadth),
    )
    lat_terms = softmax_terms(
        scores_of(key_proj[tok_count:]),
        value_proj[tok_count:].reshape(-1, subspace_number_overall, subspace_breadth),
    )
    merged = merge_all(*tok_terms)
    joint_max, joint_sum, joint_weighted = combine(merged, lat_terms)
    attention = (
        (joint_weighted / joint_sum[..., None]).transpose(1, 0, 2).reshape(lat_count, channels)
    )
    attention_low = attention.astype(jnp.bfloat16)
    out_cols = jnp.dot(attention_low, final_projection_tensor, preferred_element_type=jnp.float32)
    attended = lax.all_gather(out_cols, "wide", axis=1, tiled=True)
    new_latents = (summary_probes.astype(jnp.float32) + attended).astype(jnp.bfloat16)
    return (attended, new_latents)


def solution(mesh):
    placed = (
        P(("groups", "wide"), None, None, None),
        P(),
        P(),
        P(),
        P(),
        P("wide", None),
        P("wide", None),
        P("wide", None),
        P(None, "wide"),
        P(),
    )
    return jax.shard_map(
        per_device,
        mesh=mesh,
        in_specs=placed,
        out_specs=(P("groups", None), P("groups", None)),
        check_vma=False,
    )
```

profile of v0, /device:TPU:0, one launch (start us, length us, event | category | flops | bytes accessed | tf_op | source)
XLA Modules:
  0.0 424.6 jit_solution(6361989302038620171)
XLA Ops:
  7.2 0.7 all-gather.4.cloned.1.call-update
  8.0 0.7 all-gather.6.cloned.1.call-update
  8.7 0.0 all-reduce.3.cloned.1.call-start
  8.7 1.1 convert_reduce_fusion
  9.8 1.2 fusion.34
  11.0 1.1 fusion.36
  12.0 0.3 fusion.41
  12.3 0.2 reshape.82
  12.5 1.0 copy.42
  13.5 0.0 all-reduce.5.cloned.1.call-start
  13.5 6.2 %copy.43 = bf16[3,3,128,1536]{2,3,1,0:T(8,128)(2,1)} copy(bf16[3,3,128,1536]{3,2,1,0:T(8,128)(2,1)} %param.11) | data formatting | bytes 7077888 | tf_op args[1]
  19.7 9.5 %fusion.55 = (f32[8,10,10]{0,2,1:T(8,128)S(1)}, f32[8,10,10,1536]{3,0,2,1:T(8,128)}) fusion(bf16[3,3,128,12,128]{2,4,3,1,0:T(8,128)(2,1)} %bitcast.34, bf16[8,10,10,1536]{3,0,2,1:T(8,128)(2,1)S(1)} %copy-done.9), kind=kOutput, calls=%fused_computation.74 | convolution fusion | flops 2483453184 | bytes 10914944 | tf_op jit(solution)/shard_map/conv_general_dilated | solution.py:62
  29.2 0.1 copy.45
  29.3 0.1 copy.47
  29.5 8.7 %copy.44 = f32[8,10,10,1536]{3,2,1,0:T(8,128)} copy(f32[8,10,10,1536]{3,0,2,1:T(8,128)} %get-tuple-element.8) | data formatting | bytes 9830400 | tf_op jit(solution)/shard_map/add | solution.py:71
  38.2 0.6 multiply_reduce_fusion
  38.8 0.1 copy.48
  39.0 0.1 rsqrt.21
  39.1 6.6 %reshape.83 = f32[800,1536]{1,0:T(8,128)} reshape(f32[8,10,10,1536]{3,2,1,0:T(8,128)} %copy.44) | data formatting | bytes 9830400 | tf_op jit(solution)/shard_map/reshape | solution.py:72
  45.7 0.1 div.29
  45.9 3.1 multiply_convert_fusion
  49.0 17.4 %all-gather.4.cloned.1.call-done = bf16[1536,1536]{1,0:T(8,128)(2,1)} async-done(((bf16[96,1536]{1,0:T(8,128)(2,1)}), bf16[1536,1536]{1,0:T(8,128)(2,1)}) %all-gather.4.cloned.1.call-update) | async-done | bytes 4718608 | tf_op jit(solution)/shard_map/all_gather | solution.py:105
  66.4 8.6 %fusion.19 = f32[864,1536]{1,0:T(8,128)} fusion(bf16[1536,1536]{1,0:T(8,128)(2,1)} %all-gather.4.cloned.1.call-done, bf16[64,1536]{1,0:T(8,128)(2,1)S(1)} %fusion.36, bf16[800,1536]{1,0:T(8,128)(2,1)S(1)} %multiply_convert_fusion), kind=kOutput, calls=%fused_computation.25 | convolution fusion | flops 4082171904 | bytes 12681216 | tf_op jit(solution)/shard_map/dot_general | solution.py:93
  75.0 45.7 %all-gather.6.cloned.1.call-done = bf16[1536,1536]{1,0:T(8,128)(2,1)} async-done(((bf16[96,1536]{1,0:T(8,128)(2,1)}), bf16[1536,1536]{1,0:T(8,128)(2,1)}) %all-gather.6.cloned.1.call-update) | async-done | bytes 4718608 | tf_op jit(solution)/shard_map/all_gather | solution.py:106
  120.7 6.5 %fusion.18 = f32[864,1536]{1,0:T(8,128)S(1)} fusion(bf16[1536,1536]{1,0:T(8,128)(2,1)} %all-gather.6.cloned.1.call-done, bf16[64,1536]{1,0:T(8,128)(2,1)S(1)} %fusion.36, bf16[800,1536]{1,0:T(8,128)(2,1)S(1)} %multiply_convert_fusion), kind=kOutput, calls=%fused_computation.24 | convolution fusion | flops 4082171904 | bytes 12681216 | tf_op jit(solution)/shard_map/dot_general | solution.py:93
  127.2 2.8 slice.16
  130.0 2.5 slice.17
  132.5 6.0 %copy.50 = f32[800,1536]{0,1:T(8,128)} copy(f32[800,1536]{1,0:T(8,128)} %slice.16) | data formatting | bytes 9830400 | tf_op jit(solution)/shard_map/slice | solution.py:111
  138.5 74.2 %all-reduce.3.cloned.1.call-done = f32[64,16,96]{2,0,1:T(8,128)} async-done(((f32[64,16,96]{2,0,1:T(8,128)}), f32[64,16,96]{2,0,1:T(8,128)}) %all-reduce.3.cloned.1.call-update) | async-done | bytes 393232 | tf_op jit(solution)/shard_map/psum | solution.py:82
  212.7 8.3 %fusion.56 = (f32[16,64]{1,0:T(8,128)S(1)}, f32[16,64,800]{2,1,0:T(8,128)}) fusion(f32[800,16,96]{0,2,1:T(8,128)} %bitcast.30, f32[64,16,96]{2,0,1:T(8,128)} %all-reduce.3.cloned.1.call-done, f32[16]{0:T(128)S(1)} %broadcast_multiply_fusion.1), kind=kOutput, calls=%fused_computation.75 | convolution fusion | flops 944634880 | bytes 8589376 | tf_op jit(solution)/shard_map/lhd,thd->hlt/dot_general | solution.py:96
  221.0 32.4 %pmax.7 = f32[16,64]{1,0:T(8,128)S(1)} all-reduce(f32[16,64]{1,0:T(8,128)S(1)} %get-tuple-element.9), channel_id=1, replica_groups=mesh['groups'=2,'wide'=16] {'wide'}, use_global_device_ids=true, to_apply=%region_6.0 | all-reduce | flops 1024 | bytes 8192 | tf_op jit(solution)/shard_map/pmax | solution.py:31
  253.5 2.9 fusion.6
  256.4 30.0 %psum.23 = f32[16,64]{1,0:T(8,128)S(1)} all-reduce(f32[16,64]{1,0:T(8,128)S(1)} %get-tuple-element.5), channel_id=1, replica_groups=mesh['groups'=2,'wide'=16] {'wide'}, use_global_device_ids=true, to_apply=%region_10.0 | all-reduce | flops 1024 | bytes 8192 | tf_op jit(solution)/shard_map/psum | solution.py:33
  286.4 0.2 reshape.86
  286.6 6.0 %copy.51 = f32[800,1536]{0,1:T(8,128)} copy(f32[800,1536]{1,0:T(8,128)} %slice.17) | data formatting | bytes 9830400 | tf_op jit(solution)/shard_map/slice | solution.py:112
  292.6 11.3 %fusion.20 = f32[16,64,96]{2,1,0:T(8,128)} fusion(f32[800,16,96]{0,2,1:T(8,128)} %bitcast.31, f32[16,64,800]{2,1,0:T(8,128)} %get-tuple-element.10, f32[16,64]{1,0:T(8,128)S(1)} %get-tuple-element.9, f32[16,64]{1,0:T(8,128)S(1)} %get-tuple-element.6), kind=kOutput, calls=%fused_computation.26 | convolution fusion | flops 944635904 | bytes 8593408 | tf_op jit(solution)/shard_map/hlt,thd->hld/dot_general | solution.py:41
  303.9 0.2 reshape.87
  304.1 1.1 fusion.57
  305.2 0.1 fusion.33
  305.4 85.9 %all-reduce.5.cloned.1.call-done = f32[16,64,96]{2,1,0:T(8,128)} async-done(((f32[16,64,96]{2,1,0:T(8,128)}), f32[16,64,96]{2,1,0:T(8,128)}) %all-reduce.5.cloned.1.call-update) | async-done | bytes 393232 | tf_op jit(solution)/shard_map/psum | solution.py:33
  391.3 2.5 fusion.24
  393.8 0.2 copy.55
  393.9 0.3 convert_element_type.39
  394.2 0.2 convolution_bitcast_fusion
  394.4 22.2 %all-gather = f32[16,96,64]{1,2,0:T(8,128)S(1)} all-gather(f32[1,96,64]{1,2,0:T(8,128)S(1)} %convolution_bitcast_fusion), channel_id=1, replica_groups=mesh['groups'=2,'wide'=16] {'wide'}, dimensions={0}, use_global_device_ids=true | all-gather | bytes 417792 | tf_op jit(solution)/shard_map/all_gather | solution.py:125
  416.7 0.3 copy.56
  417.0 0.2 reshape.89
  417.2 0.8 fusion.37
  (44 shorter events, 0.3 us)
Async XLA Ops:
  7.2 4.9 %copy-start = (bf16[96,1536]{1,0:T(8,128)(2,1)S(1)}, bf16[96,1536]{1,0:T(8,128)(2,1)}, u32[]{:S(2)}) copy-start(bf16[96,1536]{1,0:T(8,128)(2,1)} %param.15) | copy-start | bytes 884740
  7.2 59.2 %all-gather.4.cloned.1.call-start = ((), (), s32[]{:S(2)}) async-start(), calls=%async_computation.1 | async-start | bytes 5013504 | tf_op jit(solution)/shard_map/all_gather | solution.py:105
  7.9 112.8 %all-gather.6.cloned.1.call-start = ((), (), s32[]{:S(2)}) async-start(), calls=%async_computation.2 | async-start | bytes 5013504 | tf_op jit(solution)/shard_map/all_gather | solution.py:106
  8.7 204.1 %all-reduce.3.cloned.1.call-start = ((), (), s32[]{:S(2)}) async-start(), calls=%async_computation | async-start | bytes 1048576 | tf_op jit(solution)/shard_map/psum | solution.py:82
  13.5 6.3 %copy-start.9 = (bf16[8,10,10,1536]{3,0,2,1:T(8,128)(2,1)S(1)}, bf16[8,10,10,1536]{3,0,2,1:T(8,128)(2,1)}, u32[]{:S(2)}) copy-start(bf16[8,10,10,1536]{3,0,2,1:T(8,128)(2,1)} %param.10) | copy-start | bytes 7372804
  13.5 377.8 %all-reduce.5.cloned.1.call-start = ((), (), s32[]{:S(2)}) async-start(), calls=%async_computation.3 | async-start | bytes 1048576 | tf_op jit(solution)/shard_map/psum | solution.py:33
  29.3 8.8 %slice-start = ((s8[4915200]{0:T(1024)(128)(4,1)}), s8[720896]{0:T(1024)(128)(4,1)S(1)}, s32[]{:S(2)}) async-start(s8[4915200]{0:T(1024)(128)(4,1)} %bitcast.32), calls=%async_computation.4 | async-start | bytes 1441792
  29.5 8.7 %slice-start.1 = ((s8[4915200]{0:T(1024)(128)(4,1)}), s8[4194304]{0:T(1024)(128)(4,1)S(1)}, s32[]{:S(2)}) async-start(s8[4915200]{0:T(1024)(128)(4,1)} %bitcast.32), calls=%async_computation.5 | async-start | bytes 8388608
  39.1 6.8 %copy-start.10 = (f32[16]{0:T(128)S(1)}, f32[16]{0:T(128)}, u32[]{:S(2)}) copy-start(f32[16]{0:T(128)} %param.19) | copy-start | bytes 196
  39.1 6.8 %copy-start.8 = (f32[1536]{0:T(1024)S(1)}, f32[1536]{0:T(1024)}, u32[]{:S(2)}) copy-start(f32[1536]{0:T(1024)} %param.12) | copy-start | bytes 18436
  120.7 6.5 %copy-start.2 = (f32[864,1536]{1,0:T(8,128)S(1)}, f32[864,1536]{1,0:T(8,128)}, u32[]{:S(2)}) copy-start(f32[864,1536]{1,0:T(8,128)} %fusion.19) | copy-start | bytes 15925252
  127.2 5.4 %copy-start.3 = (f32[864,1536]{1,0:T(8,128)}, f32[864,1536]{1,0:T(8,128)S(1)}, u32[]{:S(2)}) copy-start(f32[864,1536]{1,0:T(8,128)S(1)} %fusion.18) | copy-start | bytes 15925252
  212.7 73.7 %slice-start.2 = ((f32[864,1536]{1,0:T(8,128)}), f32[64,1536]{1,0:T(8,128)S(1)}, s32[]{:S(2)}) async-start(f32[864,1536]{1,0:T(8,128)} %fusion.19), calls=%async_computation.6 | async-start | bytes 786432 | tf_op jit(solution)/shard_map/slice | solution.py:115
  292.5 11.3 %slice-start.3 = ((f32[864,1536]{1,0:T(8,128)}), f32[64,1536]{1,0:T(8,128)S(1)}, s32[]{:S(2)}) async-start(f32[864,1536]{1,0:T(8,128)} %copy-done.3), calls=%async_computation.7 | async-start | bytes 786432 | tf_op jit(solution)/shard_map/slice | solution.py:116
  292.6 11.5 %copy-start.5 = (f32[64,16,96]{2,0,1:T(8,128)S(1)}, f32[64,16,96]{2,0,1:T(8,128)}, u32[]{:S(2)}) copy-start(f32[64,16,96]{2,0,1:T(8,128)} %all-reduce.3.cloned.1.call-done) | copy-start | bytes 1179652
  303.8 90.4 %copy-start.7 = (bf16[1536,96]{0,1:T(8,128)(2,1)S(1)}, bf16[1536,96]{0,1:T(8,128)(2,1)}, u32[]{:S(2)}) copy-start(bf16[1536,96]{0,1:T(8,128)(2,1)} %param.18) | copy-start | bytes 884740
  303.9 113.4 %copy-start.4 = (bf16[64,1536]{1,0:T(8,128)(2,1)S(1)}, bf16[64,1536]{1,0:T(8,128)(2,1)}, u32[]{:S(2)}) copy-start(bf16[64,1536]{1,0:T(8,128)(2,1)} %param.13) | copy-start | bytes 589828
  303.9 114.2 %copy-start.1 = (bf16[96,1536]{1,0:T(8,128)(2,1)S(1)}, bf16[96,1536]{1,0:T(8,128)(2,1)}, u32[]{:S(2)}) copy-start(bf16[96,1536]{1,0:T(8,128)(2,1)} %param.15) | copy-start | bytes 884740
  417.2 0.8 copy-start.6
Sparse Core Ops, SparseCore 0:
  10.3 56.0 all-gather.3
  68.7 51.9 all-gather.5
  124.1 88.5 all-reduce.2
  304.0 87.2 all-reduce.4
where the time goes:
time: 425 us
  waiting for transfers between devices  225 us (53%)
  blocking collectives  84.7 us (20%)
  matrix products  48.2 us (11%)
  local copies, waits for them, and re-layouts  42 us (10%)
  between operations  14.1 us (3%)
  other arithmetic  10.9 us (3%)
    psum x1, waiting for transfers between devices, merge_all(): lax.psum((row_sum * factor, weighted * factor[..., None]), 'wide')  85.9 us
    psum x1, waiting for transfers between devices, per_device(): lax.psum(jnp.dot(lat_slice, asking_projection_tensor, preferred_element_t...  74.2 us
    all_gather x1, waiting for transfers between devices, per_device(): lax.all_gather(content_projection_tensor, 'wide', axis=0, tiled=True)  45.7 us
    pmax x1, blocking collectives, merge_all(): joint_max = lax.pmax(row_max, 'wide')  32.4 us
    psum x1, blocking collectives, merge_all(): lax.psum((row_sum * factor, weighted * factor[..., None]), 'wide')  30 us
    all_gather x1, blocking collectives, per_device(): attended = lax.all_gather(out_cols, 'wide', axis=1, tiled=True)  22.2 us
    all_gather x1, waiting for transfers between devices, per_device(): lax.all_gather(lookup_projection_tensor, 'wide', axis=0, tiled=True)  17.4 us
    dot_general x2, matrix products, add_rows(): jnp.dot(key_source, weight_rows, preferred_element_type=jnp.float32)  15 us
  transfers between devices with their start and end apart: 4, of which 4 were waited for; matrix products, arithmetic and copies ran while one was open for 16% of the time, Pallas kernels for 0%

commit v1 on v0

--- a/solution.py
+++ b/solution.py
@@ -6,6 +6,18 @@
 
 RESIDUAL_SCALE = 0.2
 EPSILON = 1e-06
+
+
+def collect(shard, axis, dim):
+    ways, here = (lax.axis_size(axis), lax.axis_index(axis))
+    grown, reach = (shard, 1)
+    while reach < ways:
+        theirs = lax.ppermute(grown, axis, [(d, d ^ reach) for d in range(ways)])
+        mine_first = jnp.concatenate([grown, theirs], axis=dim)
+        theirs_first = jnp.concatenate([theirs, grown], axis=dim)
+        grown = jnp.where(here & reach == 0, mine_first, theirs_first)
+        reach = 2 * reach
+    return grown
 
 
 def layer_norm(values, gain):
@@ -102,7 +114,7 @@
 
     running = (zero_rows, zero_rows)
     weight_rows = (
-        lax.all_gather(lookup_projection_tensor, "wide", axis=0, tiled=True),
+        collect(lookup_projection_tensor, "wide", 0),
         lax.all_gather(content_projection_tensor, "wide", axis=0, tiled=True),
     )
     key_proj = add_rows(running[0], weight_rows[0])

time: 425 us -> 418 us (0.984)
  waiting for transfers between devices: 225 us -> 201 us
  starting transfers between devices: 0.16 us -> 7.91 us
    ppermute x0 -> x4, waiting for transfers between devices: none -> 113 us  [collect(): theirs = lax.ppermute(grown, axis, [(d, d ^ reach) for d in range(ways)])]
    psum x1, waiting for transfers between devices: 74.2 us -> 0.01 us  [per_device(): lax.psum(jnp.dot(lat_slice, asking_projection_tensor, preferred_element_t...]
    all_gather x1, waiting for transfers between devices: 45.7 us -> 0.02 us  [per_device(): lax.all_gather(content_projection_tensor, 'wide', axis=0, tiled=True)]
    all_gather x1 -> x0, waiting for transfers between devices: 17.4 us -> none  [per_device(): lax.all_gather(lookup_projection_tensor, 'wide', axis=0, tiled=True)]
    ppermute x0 -> x4, starting transfers between devices: none -> 7.79 us  [collect(): theirs = lax.ppermute(grown, axis, [(d, d ^ reach) for d in range(ways)])]
    unnamed x28 -> x30, local copies, waits for them, and re-layouts: 6.53 us -> 9.49 us
  transfers between devices with their start and end apart: 4 -> 7, of which waited for: 4 -> 5; matrix products, arithmetic and copies ran while one was open for 16% -> 17% of each run, Pallas kernels for 0% -> 0%
where the time goes in v1:
time: 418 us
  waiting for transfers between devices  201 us (48%)
  blocking collectives  86.3 us (21%)
  matrix products  47.6 us (11%)
  local copies, waits for them, and re-layouts  46.2 us (11%)
  other arithmetic  14.2 us (3%)
  between operations  14.1 us (3%)
  starting transfers between devices  7.91 us (2%)
    ppermute x4, waiting for transfers between devices, collect(): theirs = lax.ppermute(grown, axis, [(d, d ^ reach) for d in range(ways)])  113 us
    psum x1, waiting for transfers between devices, merge_all(): lax.psum((row_sum * factor, weighted * factor[..., None]), 'wide')  87.2 us
    pmax x1, blocking collectives, merge_all(): joint_max = lax.pmax(row_max, 'wide')  34 us
    psum x1, blocking collectives, merge_all(): lax.psum((row_sum * factor, weighted * factor[..., None]), 'wide')  30 us
    all_gather x1, blocking collectives, per_device(): attended = lax.all_gather(out_cols, 'wide', axis=1, tiled=True)  22.2 us
    dot_general x2, matrix products, softmax_terms(): jnp.einsum('hlt,thd->hld', weights, carried, precision=lax.Precision.HIGH...  13.7 us
    dot_general x2, matrix products, add_rows(): jnp.dot(key_source, weight_rows, preferred_element_type=jnp.float32)  13.3 us
    dot_general x2, matrix products, scores_of(): jnp.einsum('lhd,thd->hlt', rescaled_similarity_logits, key_part.reshape(-...  10.5 us
  transfers between devices with their start and end apart: 7, of which 5 were waited for; matrix products, arithmetic and copies ran while one was open for 17% of the time, Pallas kernels for 0%

profile of v1, /device:TPU:0, one launch (start us, length us, event | category | flops | bytes accessed | tf_op | source)
XLA Modules:
  0.0 417.7 jit_solution(4824030671447283107)
XLA Ops:
  7.2 1.1 convert_reduce_fusion
  8.3 1.2 fusion.40
  9.5 1.1 fusion.42
  10.6 0.3 fusion.47
  10.9 0.2 reshape.82
  11.0 0.9 copy.42
  12.1 0.7 all-gather.3.cloned.1.call-update
  12.8 0.5 collective-permute-start
  13.3 1.4 collective-permute-done
  14.7 1.2 maximum_select_fusion.4
  15.9 3.0 collective-permute-start.1
  18.9 15.2 %collective-permute-done.1 = bf16[192,1536]{1,0:T(8,128)(2,1)S(1)} collective-permute-done((bf16[192,1536]{1,0:T(8,128)(2,1)S(1)}, bf16[192,1536]{1,0:T(8,128)(2,1)S(1)}, u32[]{:S(2)}, u32[]{:S(2)}) %collective-permute-start.1) | collective-permute-done | bytes 589856 | tf_op jit(solution)/shard_map/ppermute | solution.py:15
  34.1 0.4 maximum_select_fusion.3
  34.5 1.9 collective-permute-start.2
  36.3 6.0 %copy.43 = bf16[3,3,128,1536]{2,3,1,0:T(8,128)(2,1)} copy(bf16[3,3,128,1536]{3,2,1,0:T(8,128)(2,1)} %param.11) | data formatting | bytes 7077888 | tf_op args[1]
  42.4 21.4 %collective-permute-done.2 = bf16[384,1536]{1,0:T(8,128)(2,1)S(1)} collective-permute-done((bf16[384,1536]{1,0:T(8,128)(2,1)S(1)}, bf16[384,1536]{1,0:T(8,128)(2,1)S(1)}, u32[]{:S(2)}, u32[]{:S(2)}) %collective-permute-start.2) | collective-permute-done | bytes 1179680 | tf_op jit(solution)/shard_map/ppermute | solution.py:15
  63.8 1.8 maximum_select_fusion.2
  65.6 2.5 collective-permute-start.3
  68.0 9.7 %fusion.61 = (f32[8,10,10]{0,2,1:T(8,128)S(1)}, f32[8,10,10,1536]{3,0,2,1:T(8,128)}) fusion(bf16[3,3,128,12,128]{2,4,3,1,0:T(8,128)(2,1)S(1)} %bitcast.33, bf16[8,10,10,1536]{3,0,2,1:T(8,128)(2,1)} %param.10), kind=kOutput, calls=%fused_computation.84 | convolution fusion | flops 2483453184 | bytes 10914944 | tf_op jit(solution)/shard_map/conv_general_dilated | solution.py:74
  78.0 8.7 %copy.44 = f32[8,10,10,1536]{3,2,1,0:T(8,128)} copy(f32[8,10,10,1536]{3,0,2,1:T(8,128)} %get-tuple-element.8) | data formatting | bytes 9830400 | tf_op jit(solution)/shard_map/add | solution.py:83
  86.7 0.6 multiply_reduce_fusion
  87.7 7.2 %reshape.83 = f32[800,1536]{1,0:T(8,128)} reshape(f32[8,10,10,1536]{3,2,1,0:T(8,128)} %copy.44) | data formatting | bytes 9830400 | tf_op jit(solution)/shard_map/reshape | solution.py:84
  95.0 3.1 multiply_convert_fusion
  98.1 75.3 %collective-permute-done.3 = bf16[768,1536]{1,0:T(8,128)(2,1)} collective-permute-done((bf16[768,1536]{1,0:T(8,128)(2,1)}, bf16[768,1536]{1,0:T(8,128)(2,1)}, u32[]{:S(2)}, u32[]{:S(2)}) %collective-permute-start.3) | collective-permute-done | bytes 2359328 | tf_op jit(solution)/shard_map/ppermute | solution.py:15
  173.5 7.1 %fusion.6 = f32[864,1536]{1,0:T(8,128)S(1)} fusion(bf16[768,1536]{1,0:T(8,128)(2,1)} %collective-permute-done.3, bf16[768,1536]{1,0:T(8,128)(2,1)} %maximum_select_fusion.2, pred[]{:T(512)S(6)} %eq.12, bf16[64,1536]{1,0:T(8,128)(2,1)S(1)} %fusion.42, bf16[800,1536]{1,0:T(8,128)(2,1)S(1)} %multiply_convert_fusion), kind=kOutput, calls=%fused_computation.14 | convolution fusion | flops 4103405568 | bytes 12681217 | tf_op jit(solution)/shard_map/dot_general | solution.py:105
  180.6 2.6 slice.16
  183.2 1.0 reshape.86
  184.2 6.0 %copy.50 = f32[800,1536]{0,1:T(8,128)} copy(f32[800,1536]{1,0:T(8,128)} %slice.16) | data formatting | bytes 9830400 | tf_op jit(solution)/shard_map/slice | solution.py:123
  190.2 8.3 %fusion.62 = (f32[16,64]{1,0:T(8,128)S(1)}, f32[16,64,800]{2,1,0:T(8,128)}) fusion(f32[800,16,96]{0,2,1:T(8,128)} %bitcast.29, f32[64,16,96]{2,0,1:T(8,128)} %all-reduce.3.cloned.1.call-done, f32[16]{0:T(128)S(1)} %broadcast_multiply_fusion.1), kind=kOutput, calls=%fused_computation.85 | convolution fusion | flops 944634880 | bytes 8589376 | tf_op jit(solution)/shard_map/lhd,thd->hlt/dot_general | solution.py:108
  198.5 34.0 %pmax.7 = f32[16,64]{1,0:T(8,128)S(1)} all-reduce(f32[16,64]{1,0:T(8,128)S(1)} %get-tuple-element.9), channel_id=1, replica_groups=mesh['groups'=2,'wide'=16] {'wide'}, use_global_device_ids=true, to_apply=%region_6.7 | all-reduce | flops 1024 | bytes 8192 | tf_op jit(solution)/shard_map/pmax | solution.py:43
  232.6 2.9 fusion.13
  235.5 30.0 %psum.23 = f32[16,64]{1,0:T(8,128)S(1)} all-reduce(f32[16,64]{1,0:T(8,128)S(1)} %get-tuple-element.5), channel_id=1, replica_groups=mesh['groups'=2,'wide'=16] {'wide'}, use_global_device_ids=true, to_apply=%region_10.11 | all-reduce | flops 1024 | bytes 8192 | tf_op jit(solution)/shard_map/psum | solution.py:45
  265.5 2.2 fusion.63
  267.7 0.8 copy-done.6
  268.6 6.1 %fusion.25 = f32[864,1536]{1,0:T(8,128)S(1)} fusion(bf16[1536,1536]{1,0:T(8,128)(2,1)} %all-gather.3.cloned.1.call-done, bf16[64,1536]{1,0:T(8,128)(2,1)S(1)} %fusion.42, bf16[800,1536]{1,0:T(8,128)(2,1)S(1)} %multiply_convert_fusion), kind=kOutput, calls=%fused_computation.33 | convolution fusion | flops 4082171904 | bytes 12681216 | tf_op jit(solution)/shard_map/dot_general | solution.py:105
  274.8 2.4 copy-done.2
  277.2 2.6 slice.17
  279.8 5.9 %copy.51 = f32[800,1536]{0,1:T(8,128)} copy(f32[800,1536]{1,0:T(8,128)} %slice.17) | data formatting | bytes 9830400 | tf_op jit(solution)/shard_map/slice | solution.py:124
  285.7 11.2 %fusion.26 = f32[16,64,96]{2,1,0:T(8,128)} fusion(f32[800,16,96]{0,2,1:T(8,128)} %bitcast.30, f32[16,64,800]{2,1,0:T(8,128)} %get-tuple-element.10, f32[16,64]{1,0:T(8,128)S(1)} %get-tuple-element.9, f32[16,64]{1,0:T(8,128)S(1)} %get-tuple-element.6), kind=kOutput, calls=%fused_computation.34 | convolution fusion | flops 944635904 | bytes 8593408 | tf_op jit(solution)/shard_map/hlt,thd->hld/dot_general | solution.py:53
  297.2 87.2 %all-reduce.5.cloned.1.call-done = f32[16,64,96]{2,1,0:T(8,128)} async-done(((f32[16,64,96]{2,1,0:T(8,128)}), f32[16,64,96]{2,1,0:T(8,128)}) %all-reduce.5.cloned.1.call-update) | async-done | bytes 393232 | tf_op jit(solution)/shard_map/psum | solution.py:45
  384.4 2.5 fusion.30
  386.8 0.2 copy.55
  387.0 0.3 convert_element_type.39
  387.3 0.2 convolution_bitcast_fusion
  387.5 22.2 %all-gather = f32[16,96,64]{1,2,0:T(8,128)S(1)} all-gather(f32[1,96,64]{1,2,0:T(8,128)S(1)} %convolution_bitcast_fusion), channel_id=1, replica_groups=mesh['groups'=2,'wide'=16] {'wide'}, dimensions={0}, use_global_device_ids=true | all-gather | bytes 417792 | tf_op jit(solution)/shard_map/all_gather | solution.py:137
  409.8 0.3 copy.56
  410.1 0.2 reshape.89
  410.3 0.8 fusion.43
  (53 shorter events, 1.3 us)
Async XLA Ops:
  7.2 3.4 copy-start
  7.2 183.0 %all-reduce.3.cloned.1.call-start = ((), (), s32[]{:S(2)}) async-start(), calls=%async_computation | async-start | bytes 1048576 | tf_op jit(solution)/shard_map/psum | solution.py:94
  12.0 256.6 %all-gather.3.cloned.1.call-start = ((), (), s32[]{:S(2)}) async-start(), calls=%async_computation.1 | async-start | bytes 5013504 | tf_op jit(solution)/shard_map/all_gather | solution.py:118
  12.8 371.6 %all-reduce.5.cloned.1.call-start = ((), (), s32[]{:S(2)}) async-start(), calls=%async_computation.2 | async-start | bytes 1048576 | tf_op jit(solution)/shard_map/psum | solution.py:45
  12.8 1.9 collective-permute-start
  15.9 18.2 %collective-permute-start.1 = (bf16[192,1536]{1,0:T(8,128)(2,1)S(1)}, bf16[192,1536]{1,0:T(8,128)(2,1)S(1)}, u32[]{:S(2)}, u32[]{:S(2)}) collective-permute-start(bf16[192,1536]{1,0:T(8,128)(2,1)S(1)} %maximum_select_fusion.4), channel_id=1, source_target_pairs={{0,2},{1,3},{2,0},{3,1},{4,6},{5,7},{6,4},{7,5},{8,10},{9,11},{10,... | collective-permute-start | bytes 1769480 | tf_op jit(solution)/shard_map/ppermute | solution.py:15
  34.5 29.3 %collective-permute-start.2 = (bf16[384,1536]{1,0:T(8,128)(2,1)S(1)}, bf16[384,1536]{1,0:T(8,128)(2,1)S(1)}, u32[]{:S(2)}, u32[]{:S(2)}) collective-permute-start(bf16[384,1536]{1,0:T(8,128)(2,1)S(1)} %maximum_select_fusion.3), channel_id=1, source_target_pairs={{0,4},{1,5},{2,6},{3,7},{4,0},{5,1},{6,2},{7,3},{8,12},{9,13},{10,... | collective-permute-start | bytes 3538952 | tf_op jit(solution)/shard_map/ppermute | solution.py:15
  42.4 25.7 %copy-start.3 = (bf16[3,3,128,1536]{2,3,1,0:T(8,128)(2,1)S(1)}, bf16[3,3,128,1536]{2,3,1,0:T(8,128)(2,1)}, u32[]{:S(2)}) copy-start(bf16[3,3,128,1536]{2,3,1,0:T(8,128)(2,1)} %copy.43) | copy-start | bytes 10616836
  65.6 107.9 %collective-permute-start.3 = (bf16[768,1536]{1,0:T(8,128)(2,1)}, bf16[768,1536]{1,0:T(8,128)(2,1)}, u32[]{:S(2)}, u32[]{:S(2)}) collective-permute-start(bf16[768,1536]{1,0:T(8,128)(2,1)} %maximum_select_fusion.2), channel_id=1, source_target_pairs={{0,8},{1,9},{2,10},{3,11},{4,12},{5,13},{6,14},{7,15},{8,0},{9,1},... | collective-permute-start | bytes 7077896 | tf_op jit(solution)/shard_map/ppermute | solution.py:15
  77.9 8.8 %slice-start = ((s8[4915200]{0:T(1024)(128)(4,1)}), s8[720896]{0:T(1024)(128)(4,1)S(1)}, s32[]{:S(2)}) async-start(s8[4915200]{0:T(1024)(128)(4,1)} %bitcast.31), calls=%async_computation.3 | async-start | bytes 1441792
  78.0 8.7 %slice-start.1 = ((s8[4915200]{0:T(1024)(128)(4,1)}), s8[4194304]{0:T(1024)(128)(4,1)S(1)}, s32[]{:S(2)}) async-start(s8[4915200]{0:T(1024)(128)(4,1)} %bitcast.31), calls=%async_computation.4 | async-start | bytes 8388608
  87.6 7.4 %copy-start.11 = (f32[16]{0:T(128)S(1)}, f32[16]{0:T(128)}, u32[]{:S(2)}) copy-start(f32[16]{0:T(128)} %param.19) | copy-start | bytes 196
  87.6 7.4 %copy-start.10 = (f32[1536]{0:T(1024)S(1)}, f32[1536]{0:T(1024)}, u32[]{:S(2)}) copy-start(f32[1536]{0:T(1024)} %param.12) | copy-start | bytes 18436
  190.2 75.3 %copy-start.5 = (f32[64,16,96]{2,0,1:T(8,128)S(1)}, f32[64,16,96]{2,0,1:T(8,128)}, u32[]{:S(2)}) copy-start(f32[64,16,96]{2,0,1:T(8,128)} %all-reduce.3.cloned.1.call-done) | copy-start | bytes 1179652
  267.7 0.8 copy-start.6
  274.8 2.4 copy-start.2
  285.7 11.3 %slice-start.2 = ((f32[864,1536]{1,0:T(8,128)}), f32[64,1536]{1,0:T(8,128)S(1)}, s32[]{:S(2)}) async-start(f32[864,1536]{1,0:T(8,128)} %copy-done.2), calls=%async_computation.5 | async-start | bytes 786432 | tf_op jit(solution)/shard_map/slice | solution.py:128
  285.7 98.7 %copy-start.7 = (f32[16,64,64]{1,2,0:T(8,128)S(1)}, f32[16,64,64]{1,2,0:T(8,128)}, u32[]{:S(2)}) copy-start(f32[16,64,64]{1,2,0:T(8,128)} %copy-done.6) | copy-start | bytes 786436
  297.0 90.3 %copy-start.9 = (bf16[1536,96]{0,1:T(8,128)(2,1)S(1)}, bf16[1536,96]{0,1:T(8,128)(2,1)}, u32[]{:S(2)}) copy-start(bf16[1536,96]{0,1:T(8,128)(2,1)} %param.18) | copy-start | bytes 884740
  297.0 113.3 %copy-start.4 = (bf16[64,1536]{1,0:T(8,128)(2,1)S(1)}, bf16[64,1536]{1,0:T(8,128)(2,1)}, u32[]{:S(2)}) copy-start(bf16[64,1536]{1,0:T(8,128)(2,1)} %param.13) | copy-start | bytes 589828
  297.0 114.1 %copy-start.1 = (bf16[96,1536]{1,0:T(8,128)(2,1)S(1)}, bf16[96,1536]{1,0:T(8,128)(2,1)}, u32[]{:S(2)}) copy-start(bf16[96,1536]{1,0:T(8,128)(2,1)} %param.15) | copy-start | bytes 884740
  410.3 0.8 copy-start.8
Sparse Core Ops, SparseCore 0:
  12.1 163.1 all-reduce.2
  177.6 53.6 all-gather.2
  297.1 87.2 all-reduce.4
